TPU v7x, 512 devices: a whole 4x4x16 slice. The times are simulated.
512 devices in a mesh: space: 64 (over z_lo, x, core), batch: 8 (over z_hi, y).
Axes of the slice: x: 4, y: 4, z: 16 (z_hi: 2, z_lo: 8; z = z_hi * 8 + z_lo), core: 2. Of those that a mesh axis runs over, the one named last changes fastest.
Arguments:
- fine_parts: bfloat16 [8, 32768, 128], P('batch', 'space'), may hold values from -5 to 5
- parent_parts: bfloat16 [8, 4096, 128], P('batch', 'space'), may hold values from -5 to 5
- coarse_local: float32 [4096, 128], P('space'), may hold values from -6 to 6
- fine_source: int32 [189, 32768], P(None, 'space'), may hold values from 0 to 159
- fine_operator: int32 [189, 32768], P(None, 'space'), may hold values from 0 to 63
- parent_source: int32 [189, 4096], P(None, 'space'), may hold values from 0 to 159
- parent_operator: int32 [189, 4096], P(None, 'space'), may hold values from 0 to 63
- operators: bfloat16 [64, 128, 128], replicated, may hold values from -0.0390625 to 0.0390625
- child_shift: bfloat16 [8, 128, 128], replicated, may hold values from -0.5 to 0.5
- basis: bfloat16 [32768, 128, 128], P('space', 'batch'), may hold values from -0.5 to 0.5
- counts: int32 [8, 32768], P('batch', 'space'), may hold values from 1 to 16
Outputs:
- potential: float32 [128, 32768], P('batch', 'space')
Inputs may be any that keep to these rules, and one draw needn't show every extreme that they name: `fine_source`: an entry v names, in the target's own block if v // 32 is 0 and else in the block whose index differs from the target's in bit v // 32 - 1, box v % 32 of the aligned group of 32 boxes that holds the target's position. `parent_source`: an entry v names, in the target's own block if v // 32 is 0 and else in the block whose index differs from the target's in bit v // 32 - 1, parent box v % 32 of the aligned group of 32 parent boxes that holds the target's position.
All inputs are finite; a program needn't handle non-finite values.
Results may differ from a plain program's by a relative error of at most 0.015.
Values may be sent and summed in bfloat16 or wider, within the bound.
A program may use at most 64 MiB of HBM per device.

v0:
```python
import math
import jax
import jax.numpy as jnp
from jax import lax
from jax.sharding import PartitionSpec as P

NTERMS = 121
WINDOW = 32


def partner(shard, axis, apart):
    return lax.ppermute(shard, axis, [(i, i ^ 1 << apart) for i in range(lax.axis_size(axis))])


def far_field(stacked, source_list, operator_list, operators, row_start):
    kind_count, coef_width, _ = operators.shape
    flat_ops = operators.reshape(kind_count * coef_width, coef_width)
    list_length, total_rows = source_list.shape
    piece_rows = math.gcd(total_rows, WINDOW)
    piece_count = total_rows // piece_rows
    source_pieces = source_list.reshape(list_length, piece_count, piece_rows).transpose(1, 0, 2)
    kind_pieces = operator_list.reshape(list_length, piece_count, piece_rows).transpose(1, 0, 2)
    starts = row_start + lax.iota(jnp.int32, piece_count) * piece_rows
    kinds_iota = lax.iota(jnp.int32, kind_count)
    column_iota = lax.iota(jnp.int32, stacked.shape[0] * WINDOW)

    def one_piece(pieces):
        sources, kinds, start = pieces
        corner = start // WINDOW * WINDOW
        nearby = lax.dynamic_slice_in_dim(stacked, corner, WINDOW, 1).reshape(-1, coef_width)
        chosen = (sources[:, :, None] == column_iota).astype(jnp.bfloat16)
        onehot = (kinds[:, :, None] == kinds_iota).astype(jnp.bfloat16)
        counted = jnp.einsum(
            "jbt,jbr->btr", onehot, chosen, preferred_element_type=jnp.float32
        ).astype(jnp.bfloat16)
        grouped = jnp.einsum(
            "btr,rk->btk", counted, nearby, preferred_element_type=jnp.float32
        ).astype(jnp.bfloat16)
        return jnp.dot(
            grouped.reshape(piece_rows, kind_count * coef_width),
            flat_ops,
            preferred_element_type=jnp.float32,
        )

    return lax.map(one_piece, (source_pieces, kind_pieces, starts)).reshape(total_rows, coef_width)


def with_partners(fine_mult, parent_mult):
    fine_blocks = [fine_mult]
    parent_blocks = [parent_mult]
    for bit_number in range(4):
        fine_other, parent_other = partner((fine_mult, parent_mult), "space", bit_number)
        fine_blocks.append(fine_other)
        parent_blocks.append(parent_other)
    return (jnp.stack(fine_blocks), jnp.stack(parent_blocks))


def children(parent_local, fine_far, child_shift):
    shifted = jnp.einsum(
        "pk,okl->pol", parent_local, child_shift, preferred_element_type=jnp.float32
    )
    whole = shifted.reshape(fine_far.shape) + fine_far
    keep = lax.iota(jnp.int32, whole.shape[1]) < NTERMS
    return jnp.where(keep[None, :], whole, 0.0).astype(jnp.bfloat16)


def body(
    fine_parts,
    parent_parts,
    coarse_local,
    fine_source,
    fine_operator,
    parent_source,
    parent_operator,
    operators,
    child_shift,
    basis,
    counts,
):
    fine_terms = fine_parts[0].astype(jnp.float32)
    parent_terms = parent_parts[0].astype(jnp.float32)
    fine_total, parent_total = (
        lax.psum(fine_terms.astype(jnp.bfloat16), "batch").astype(jnp.float32),
        lax.psum(parent_terms.astype(jnp.bfloat16), "batch").astype(jnp.float32),
    )
    fine_stack, parent_stack = with_partners(
        fine_total.astype(jnp.bfloat16), parent_total.astype(jnp.bfloat16)
    )
    fine_far = far_field(fine_stack, fine_source, fine_operator, operators, 0)
    parent_far = far_field(parent_stack, parent_source, parent_operator, operators, 0)
    parent_local = (coarse_local + parent_far).astype(jnp.bfloat16)
    local = children(parent_local, fine_far, child_shift)
    values = lax.dot_general(
        basis, local, (((2,), (1,)), ((0,), (0,))), preferred_element_type=jnp.float32
    ).T
    slot_index = lax.iota(jnp.int32, values.shape[0])[:, None]
    return jnp.where(slot_index < counts, values, 0.0)


def solution(mesh):
    placed = (
        P("batch", "space", None),
        P("batch", "space", None),
        P("space", None),
        P(None, "space"),
        P(None, "space"),
        P(None, "space"),
        P(None, "space"),
        P(),
        P(),
        P("space", "batch", None),
        P("batch", "space"),
    )
    return jax.shard_map(
        body, mesh=mesh, in_specs=placed, out_specs=P("batch", "space"), check_vma=False
    )
```

profile of v0, /device:TPU:1, one launch (start us, length us, event | category | flops | bytes accessed | tf_op | source)
XLA Modules:
  0.0 527.7 jit_solution(15219592119479312412)
XLA Ops:
  6.5 75.3 %psum.14 = bf16[64,128]{1,0:T(8,128)(2,1)S(1)} all-reduce(bf16[64,128]{1,0:T(8,128)(2,1)} %bitcast.139), channel_id=1, replica_groups=mesh['space'=64,'batch'=8] {'batch'}, use_global_device_ids=true, to_apply=%region_0.0 | all-reduce | flops 8192 | bytes 32768 | tf_op jit(solution)/shard_map/psum | solution.py:84
  81.9 9.8 %collective-permute-start = (bf16[64,128]{1,0:T(8,128)(2,1)S(1)}, bf16[64,128]{1,0:T(8,128)(2,1)S(1)}, u32[]{:S(2)}, u32[]{:S(2)}) collective-permute-start(bf16[64,128]{1,0:T(8,128)(2,1)S(1)} %psum.14), channel_id=1, source_target_pairs={{0,8},{8,0},{16,24},{24,16},{32,40},{40,32},{48,56},{56,48},{64,72... | collective-permute-start | bytes 49160 | tf_op jit(solution)/shard_map/ppermute | solution.py:12
  91.7 3.1 collective-permute-start.1
  94.8 4.4 collective-permute-start.2
  107.1 29.9 %while.26 = (s32[]{:T(128)}, f32[2,32,128]{2,1,0:T(8,128)}, s32[2,189,32]{1,2,0:T(8,128)}, s32[2,189,32]{1,2,0:T(8,128)}, s32[2]{0:T(128)}, /*index=5*/bf16[5,64...) while((s32[]{:T(128)}, f32[2,32,128]{2,1,0:T(8,128)}, ...), condition=%wide.region_2.3_spmd.clone, body=%wide.region_1.0_spmd.clone.sunk | while | flops 276802560 | bytes 6237277 | solution.py:45
  115.4 3.9 fusion.82
  119.3 2.8 fusion.83
  130.3 3.9 fusion.82
  134.2 2.8 fusion.83
  139.6 97.3 %all-reduce.2.cloned.1.call-done = bf16[512,128]{1,0:T(8,128)(2,1)} async-done(((bf16[512,128]{1,0:T(8,128)(2,1)}), bf16[512,128]{1,0:T(8,128)(2,1)}) %all-reduce.2.cloned.1.call-update) | async-done | bytes 131088 | tf_op jit(solution)/shard_map/psum | solution.py:83
  236.8 8.0 %collective-permute-start.4 = (bf16[512,128]{1,0:T(8,128)(2,1)}, bf16[512,128]{1,0:T(8,128)(2,1)S(1)}, u32[]{:S(2)}, u32[]{:S(2)}) collective-permute-start(bf16[512,128]{1,0:T(8,128)(2,1)} %all-reduce.2.cloned.1.call-done), channel_id=1, source_target_pairs={{0,8},{8,0},{16,24},{24,16},{32,40},{40,32},{48,56},{56,48},{64,72... | collective-permute-start | bytes 393224 | tf_op jit(solution)/shard_map/ppermute | solution.py:12
  244.9 3.1 collective-permute-start.5
  248.0 4.3 collective-permute-start.6
  259.6 258.1 %while.27 = (s32[]{:T(128)}, f32[16,32,128]{2,1,0:T(8,128)}, s32[16,189,32]{1,2,0:T(8,128)}, s32[16,189,32]{1,2,0:T(8,128)}, s32[16]{0:T(128)}, /*index=5*/bf16[...) while((s32[]{:T(128)}, f32[16,32,128]{2,1,0:T(8,128)}, ...), condition=%wide.region_5.6_spmd.clone, body=%wide.region_4.5_spmd.clone.sunk | while | flops 276802560 | bytes 6237277 | solution.py:45
  269.0 3.9 fusion.89
  285.1 3.9 fusion.89
  301.3 3.9 fusion.89
  317.4 3.9 fusion.89
  333.5 3.9 fusion.89
  349.7 3.9 fusion.89
  365.8 3.9 fusion.89
  381.9 3.9 fusion.89
  398.1 3.9 fusion.89
  414.2 3.9 fusion.89
  430.3 3.9 fusion.89
  446.5 3.9 fusion.89
  450.4 2.8 fusion.90
  462.6 3.9 fusion.89
  478.7 3.9 fusion.89
  494.9 3.9 fusion.89
  511.0 3.9 fusion.89
  515.0 2.8 fusion.90
  (181 shorter events, 180.7 us)
Async XLA Ops:
  6.5 512.4 %copy-start = (bf16[512,16,128]{2,1,0:T(8,128)(2,1)S(1)}, bf16[512,16,128]{2,1,0:T(8,128)(2,1)}, u32[]{:S(2)}) copy-start(bf16[512,16,128]{2,1,0:T(8,128)(2,1)} %param.24) | copy-start | bytes 6291460
  6.5 230.3 %all-reduce.2.cloned.1.call-start = ((), (), s32[]{:S(2)}) async-start(), calls=%async_computation | async-start | bytes 262144 | tf_op jit(solution)/shard_map/psum | solution.py:83
  81.9 25.1 %collective-permute-start = (bf16[64,128]{1,0:T(8,128)(2,1)S(1)}, bf16[64,128]{1,0:T(8,128)(2,1)S(1)}, u32[]{:S(2)}, u32[]{:S(2)}) collective-permute-start(bf16[64,128]{1,0:T(8,128)(2,1)S(1)} %psum.14), channel_id=1, source_target_pairs={{0,8},{8,0},{16,24},{24,16},{32,40},{40,32},{48,56},{56,48},{64,72... | collective-permute-start | bytes 49160 | tf_op jit(solution)/shard_map/ppermute | solution.py:12
  91.7 15.3 %collective-permute-start.1 = (bf16[64,128]{1,0:T(8,128)(2,1)S(1)}, bf16[64,128]{1,0:T(8,128)(2,1)S(1)}, u32[]{:S(2)}, u32[]{:S(2)}) collective-permute-start(bf16[64,128]{1,0:T(8,128)(2,1)S(1)} %psum.14), channel_id=1, source_target_pairs={{0,16},{8,24},{16,0},{24,8},{32,48},{40,56},{48,32},{56,40},{64,80... | collective-permute-start | bytes 49160 | tf_op jit(solution)/shard_map/ppermute | solution.py:12
  94.8 12.2 %collective-permute-start.2 = (bf16[64,128]{1,0:T(8,128)(2,1)S(1)}, bf16[64,128]{1,0:T(8,128)(2,1)S(1)}, u32[]{:S(2)}, u32[]{:S(2)}) collective-permute-start(bf16[64,128]{1,0:T(8,128)(2,1)S(1)} %psum.14), channel_id=1, source_target_pairs={{0,32},{8,40},{16,48},{24,56},{32,0},{40,8},{48,16},{56,24},{64,96... | collective-permute-start | bytes 49160 | tf_op jit(solution)/shard_map/ppermute | solution.py:12
  99.2 7.9 %collective-permute-start.3 = (bf16[64,128]{1,0:T(8,128)(2,1)S(1)}, bf16[64,128]{1,0:T(8,128)(2,1)S(1)}, u32[]{:S(2)}, u32[]{:S(2)}) collective-permute-start(bf16[64,128]{1,0:T(8,128)(2,1)S(1)} %psum.14), channel_id=1, source_target_pairs={{0,64},{8,72},{16,80},{24,88},{32,96},{40,104},{48,112},{56,120},{... | collective-permute-start | bytes 49160 | tf_op jit(solution)/shard_map/ppermute | solution.py:12
  107.1 29.9 %copy-start.1 = (f32[64,128]{1,0:T(8,128)S(1)}, f32[64,128]{1,0:T(8,128)}, u32[]{:S(2)}) copy-start(f32[64,128]{1,0:T(8,128)} %param.17) | copy-start | bytes 98308
  236.8 19.3 %collective-permute-start.4 = (bf16[512,128]{1,0:T(8,128)(2,1)}, bf16[512,128]{1,0:T(8,128)(2,1)S(1)}, u32[]{:S(2)}, u32[]{:S(2)}) collective-permute-start(bf16[512,128]{1,0:T(8,128)(2,1)} %all-reduce.2.cloned.1.call-done), channel_id=1, source_target_pairs={{0,8},{8,0},{16,24},{24,16},{32,40},{40,32},{48,56},{56,48},{64,72... | collective-permute-start | bytes 393224 | tf_op jit(solution)/shard_map/ppermute | solution.py:12
  244.9 11.9 %collective-permute-start.5 = (bf16[512,128]{1,0:T(8,128)(2,1)}, bf16[512,128]{1,0:T(8,128)(2,1)S(1)}, u32[]{:S(2)}, u32[]{:S(2)}) collective-permute-start(bf16[512,128]{1,0:T(8,128)(2,1)} %all-reduce.2.cloned.1.call-done), channel_id=1, source_target_pairs={{0,16},{8,24},{16,0},{24,8},{32,48},{40,56},{48,32},{56,40},{64,80... | collective-permute-start | bytes 393224 | tf_op jit(solution)/shard_map/ppermute | solution.py:12
  248.0 9.5 %collective-permute-start.6 = (bf16[512,128]{1,0:T(8,128)(2,1)}, bf16[512,128]{1,0:T(8,128)(2,1)S(1)}, u32[]{:S(2)}, u32[]{:S(2)}) collective-permute-start(bf16[512,128]{1,0:T(8,128)(2,1)} %all-reduce.2.cloned.1.call-done), channel_id=1, source_target_pairs={{0,32},{8,40},{16,48},{24,56},{32,0},{40,8},{48,16},{56,24},{64,96... | collective-permute-start | bytes 393224 | tf_op jit(solution)/shard_map/ppermute | solution.py:12
  252.3 6.6 %collective-permute-start.7 = (bf16[512,128]{1,0:T(8,128)(2,1)}, bf16[512,128]{1,0:T(8,128)(2,1)S(1)}, u32[]{:S(2)}, u32[]{:S(2)}) collective-permute-start(bf16[512,128]{1,0:T(8,128)(2,1)} %all-reduce.2.cloned.1.call-done), channel_id=1, source_target_pairs={{0,64},{8,72},{16,80},{24,88},{32,96},{40,104},{48,112},{56,120},{... | collective-permute-start | bytes 393224 | tf_op jit(solution)/shard_map/ppermute | solution.py:12
  517.7 2.5 copy-start.2
Sparse Core Ops, SparseCore 0:
  102.0 134.8 all-reduce.1
where the time goes:
time: 532 us; the launch traced here: 528 us
  matrix products  123 us (23%)
  waiting for transfers between devices  98 us (18%)
  blocking collectives  75.3 us (14%)
  other arithmetic  72.8 us (14%)
  local copies, waits for them, and re-layouts  60.8 us (11%)
  loops' own time  46.5 us (9%)
  starting transfers between devices  37.6 us (7%)
  between operations  13.5 us (3%)
    psum x1, waiting for transfers between devices, body(): lax.psum(fine_terms.astype(jnp.bfloat16), 'batch').astype(jnp.float32)  97.3 us
    psum x1, blocking collectives, body(): lax.psum(parent_terms.astype(jnp.bfloat16), 'batch').astype(jnp.float32)  75.3 us
    dot_general x18, matrix products, one_piece(): jnp.einsum('btr,rk->btk', counted, nearby, preferred_element_type=jnp.flo...  70.7 us
    dot_general x18, matrix products, one_piece(): jnp.dot(grouped.reshape(piece_rows, kind_count * coef_width), flat_ops, p...  49.5 us
    another operation x2, loops' own time, far_field(): lax.map(one_piece, (source_pieces, kind_pieces, starts))  46.5 us
    eq x18, other arithmetic, one_piece(): chosen = (sources[:, :, None] == column_iota).astype(jnp.bfloat16)  42.6 us
    dynamic_slice x72, local copies, waits for them, and re-layouts, far_field(): lax.map(one_piece, (source_pieces, kind_pieces, starts))  39.7 us
    ppermute x8, starting transfers between devices, partner(): lax.ppermute(shard, axis, [(i, i ^ 1 << apart) for i in range(lax.axis_si...  37.6 us
  transfers between devices with their start and end apart: 9, of which 2 were waited for; matrix products, arithmetic and copies ran while one was open for 7% of the time, Pallas kernels for 0%

commit v1 on v0

--- a/solution.py
+++ b/solution.py
@@ -6,6 +6,12 @@
 
 NTERMS = 121
 WINDOW = 32
+
+
+def summed_here(block, axis):
+    pieces = lax.all_gather(block, axis, axis=0, tiled=False)
+    total = pieces.sum(axis=0)
+    return total
 
 
 def partner(shard, axis, apart):
@@ -81,7 +87,7 @@
     parent_terms = parent_parts[0].astype(jnp.float32)
     fine_total, parent_total = (
         lax.psum(fine_terms.astype(jnp.bfloat16), "batch").astype(jnp.float32),
-        lax.psum(parent_terms.astype(jnp.bfloat16), "batch").astype(jnp.float32),
+        summed_here(parent_terms.astype(jnp.bfloat16), "batch").astype(jnp.float32),
     )
     fine_stack, parent_stack = with_partners(
         fine_total.astype(jnp.bfloat16), parent_total.astype(jnp.bfloat16)

time: 532 us -> 416 us (0.78)
  other arithmetic: 72.8 us -> 1.82 us
  matrix products: 123 us -> 82.7 us
  waiting for transfers between devices: 98 us -> 128 us
  local copies, waits for them, and re-layouts: 60.8 us -> 41.1 us
  blocking collectives: 75.3 us -> 62.1 us
    psum x1 -> x0, blocking collectives: 75.3 us -> none  [body(): lax.psum(parent_terms.astype(jnp.bfloat16), 'batch').astype(jnp.float32)]
    eq x36 -> x0, other arithmetic: 69 us -> none  [the longest x18 42.6 us: one_piece(): chosen = (sources[:, :, None] == column_iota).astype(jnp.bfloat16)]
    all_gather x0 -> x1, blocking collectives: none -> 62.1 us  [summed_here(): pieces = lax.all_gather(block, axis, axis=0, tiled=False)]
    dot_general x18, matrix products: 70.7 us -> 31.5 us  [one_piece(): jnp.einsum('btr,rk->btk', counted, nearby, preferred_element_type=jnp.flo...]
    dynamic_slice x72 -> x18, local copies, waits for them, and re-layouts: 39.7 us -> 11 us  [far_field(): lax.map(one_piece, (source_pieces, kind_pieces, starts))]
    psum x1, waiting for transfers between devices: 97.3 us -> 125 us  [body(): lax.psum(fine_terms.astype(jnp.bfloat16), 'batch').astype(jnp.float32)]
    eq x0 -> x18, local copies, waits for them, and re-layouts: none -> 12.2 us  [one_piece(): chosen = (sources[:, :, None] == column_iota).astype(jnp.bfloat16)]
  transfers between devices with their start and end apart: 9 -> 9, of which waited for: 2 -> 3; matrix products, arithmetic and copies ran while one was open for 7% -> 4% of each run, Pallas kernels for 0% -> 0%
where the time goes in v1:
time: 416 us; the launch traced here: 412 us
  waiting for transfers between devices  128 us (31%)
  matrix products  82.7 us (20%)
  blocking collectives  62.1 us (15%)
  loops' own time  46.3 us (11%)
  local copies, waits for them, and re-layouts  41.1 us (10%)
  starting transfers between devices  36.7 us (9%)
  between operations  13.7 us (3%)
    psum x1, waiting for transfers between devices, body(): lax.psum(fine_terms.astype(jnp.bfloat16), 'batch').astype(jnp.float32)  125 us
    all_gather x1, blocking collectives, summed_here(): pieces = lax.all_gather(block, axis, axis=0, tiled=False)  62.1 us
    dot_general x18, matrix products, one_piece(): jnp.dot(grouped.reshape(piece_rows, kind_count * coef_width), flat_ops, p...  49 us
    another operation x2, loops' own time, far_field(): lax.map(one_piece, (source_pieces, kind_pieces, starts))  46.3 us
    ppermute x8, starting transfers between devices, partner(): lax.ppermute(shard, axis, [(i, i ^ 1 << apart) for i in range(lax.axis_si...  36.7 us
    dot_general x18, matrix products, one_piece(): jnp.einsum('btr,rk->btk', counted, nearby, preferred_element_type=jnp.flo...  31.5 us
    dynamic_slice x18, local copies, waits for them, and re-layouts, one_piece(): lax.dynamic_slice_in_dim(stacked, corner, WINDOW, 1).reshape(-1, coef_width)  12.7 us
    eq x18, local copies, waits for them, and re-layouts, one_piece(): chosen = (sources[:, :, None] == column_iota).astype(jnp.bfloat16)  12.2 us
  transfers between devices with their start and end apart: 9, of which 3 were waited for; matrix products, arithmetic and copies ran while one was open for 4% of the time, Pallas kernels for 0%

profile of v1, /device:TPU:1, one launch (start us, length us, event | category | flops | bytes accessed | tf_op | source)
XLA Modules:
  0.0 412.3 jit_solution(13964141991496572577)
XLA Ops:
  6.5 62.1 %all_gather.4 = bf16[8,64,128]{2,1,0:T(8,128)(2,1)S(1)} all-gather(bf16[1,64,128]{2,1,0:T(8,128)(2,1)} %param.16), channel_id=1, replica_groups=mesh['space'=64,'batch'=8] {'batch'}, dimensions={0}, use_global_device_ids=true | all-gather | bytes 147456 | tf_op jit(solution)/shard_map/all_gather | solution.py:12
  68.6 10.1 %collective-permute-start = (bf16[64,128]{1,0:T(8,128)(2,1)S(1)}, bf16[64,128]{1,0:T(8,128)(2,1)S(1)}, u32[]{:S(2)}, u32[]{:S(2)}) collective-permute-start(bf16[64,128]{1,0:T(8,128)(2,1)S(1)} %reduce_sum.12), channel_id=1, source_target_pairs={{0,8},{8,0},{16,24},{24,16},{32,40},{40,32},{48,56},{56,48},{64,72... | collective-permute-start | bytes 49160 | tf_op jit(solution)/shard_map/ppermute | solution.py:18
  78.7 1.9 collective-permute-start.1
  80.7 4.3 %collective-permute-start.2 = (bf16[64,128]{1,0:T(8,128)(2,1)S(1)}, bf16[64,128]{1,0:T(8,128)(2,1)S(1)}, u32[]{:S(2)}, u32[]{:S(2)}) collective-permute-start(bf16[64,128]{1,0:T(8,128)(2,1)S(1)} %reduce_sum.12), channel_id=1, source_target_pairs={{0,32},{8,40},{16,48},{24,56},{32,0},{40,8},{48,16},{56,24},{64,96... | collective-permute-start | bytes 49160 | tf_op jit(solution)/shard_map/ppermute | solution.py:18
  85.0 2.7 collective-permute-start.3
  89.0 2.0 copy.21
  91.1 14.3 %while.26 = (s32[]{:T(128)}, f32[2,32,128]{2,1,0:T(8,128)S(1)}, s32[2,189,32]{1,2,0:T(8,128)S(1)}, s32[2,189,32]{1,2,0:T(8,128)S(1)}, s32[2]{0:T(128)S(1)}, /*in...) while((s32[]{:T(128)}, f32[2,32,128]{2,1,0:T(8,128)S(1)}, ...), condition=%wide.region_2.3_spmd.clone, body=%wide.region_1.0_spmd.clone.sunk | while | flops 276802560 | bytes 3430497 | solution.py:51
  96.0 2.2 fusion.55
  103.2 2.2 fusion.55
  106.5 124.6 %all-reduce.2.cloned.1.call-done = bf16[512,128]{1,0:T(8,128)(2,1)} async-done(((bf16[512,128]{1,0:T(8,128)(2,1)}), bf16[512,128]{1,0:T(8,128)(2,1)}) %all-reduce.2.cloned.1.call-update) | async-done | bytes 131088 | tf_op jit(solution)/shard_map/psum | solution.py:89
  231.1 8.0 %collective-permute-start.4 = (bf16[512,128]{1,0:T(8,128)(2,1)}, bf16[512,128]{1,0:T(8,128)(2,1)S(1)}, u32[]{:S(2)}, u32[]{:S(2)}) collective-permute-start(bf16[512,128]{1,0:T(8,128)(2,1)} %all-reduce.2.cloned.1.call-done), channel_id=1, source_target_pairs={{0,8},{8,0},{16,24},{24,16},{32,40},{40,32},{48,56},{56,48},{64,72... | collective-permute-start | bytes 393224 | tf_op jit(solution)/shard_map/ppermute | solution.py:18
  239.2 3.1 collective-permute-start.5
  242.3 4.3 %collective-permute-start.6 = (bf16[512,128]{1,0:T(8,128)(2,1)}, bf16[512,128]{1,0:T(8,128)(2,1)S(1)}, u32[]{:S(2)}, u32[]{:S(2)}) collective-permute-start(bf16[512,128]{1,0:T(8,128)(2,1)} %all-reduce.2.cloned.1.call-done), channel_id=1, source_target_pairs={{0,32},{8,40},{16,48},{24,56},{32,0},{40,8},{48,16},{56,24},{64,96... | collective-permute-start | bytes 393224 | tf_op jit(solution)/shard_map/ppermute | solution.py:18
  246.6 2.3 collective-permute-start.7
  251.3 1.8 collective-permute-done.7
  254.0 148.4 %while.27 = (s32[]{:T(128)}, f32[16,32,128]{2,1,0:T(8,128)}, s32[16,189,32]{1,2,0:T(8,128)S(1)}, s32[16,189,32]{1,2,0:T(8,128)}, s32[16]{0:T(128)S(1)}, /*index=...) while((s32[]{:T(128)}, f32[16,32,128]{2,1,0:T(8,128)}, ...), condition=%wide.region_5.6_spmd.clone, body=%wide.region_4.5_spmd.clone.sunk | while | flops 276802560 | bytes 3431005 | solution.py:51
  260.5 2.8 fusion.60
  269.8 2.8 fusion.60
  279.1 2.8 fusion.60
  288.3 2.8 fusion.60
  297.6 2.8 fusion.60
  306.9 2.8 fusion.60
  316.2 2.8 fusion.60
  325.4 2.8 fusion.60
  334.7 2.8 fusion.60
  344.0 2.8 fusion.60
  353.2 2.8 fusion.60
  362.5 2.8 fusion.60
  371.8 2.8 fusion.60
  381.1 2.8 fusion.60
  390.3 2.8 fusion.60
  399.6 2.8 fusion.60
  (116 shorter events, 76.2 us)
Async XLA Ops:
  6.5 397.0 %copy-start = (bf16[512,16,128]{2,1,0:T(8,128)(2,1)S(1)}, bf16[512,16,128]{2,1,0:T(8,128)(2,1)}, u32[]{:S(2)}) copy-start(bf16[512,16,128]{2,1,0:T(8,128)(2,1)} %param.24) | copy-start | bytes 6291460
  6.5 84.5 %copy-start.1 = (s32[189,64]{0,1:T(8,128)S(1)}, s32[189,64]{0,1:T(8,128)}, u32[]{:S(2)}) copy-start(s32[189,64]{0,1:T(8,128)} %param.21) | copy-start | bytes 145156
  6.5 84.5 %copy-start.2 = (s32[189,64]{0,1:T(8,128)S(1)}, s32[189,64]{0,1:T(8,128)}, u32[]{:S(2)}) copy-start(s32[189,64]{0,1:T(8,128)} %param.20) | copy-start | bytes 145156
  6.5 224.6 %all-reduce.2.cloned.1.call-start = ((), (), s32[]{:S(2)}) async-start(), calls=%async_computation | async-start | bytes 262144 | tf_op jit(solution)/shard_map/psum | solution.py:89
  68.6 22.3 %collective-permute-start = (bf16[64,128]{1,0:T(8,128)(2,1)S(1)}, bf16[64,128]{1,0:T(8,128)(2,1)S(1)}, u32[]{:S(2)}, u32[]{:S(2)}) collective-permute-start(bf16[64,128]{1,0:T(8,128)(2,1)S(1)} %reduce_sum.12), channel_id=1, source_target_pairs={{0,8},{8,0},{16,24},{24,16},{32,40},{40,32},{48,56},{56,48},{64,72... | collective-permute-start | bytes 49160 | tf_op jit(solution)/shard_map/ppermute | solution.py:18
  78.7 12.2 %collective-permute-start.1 = (bf16[64,128]{1,0:T(8,128)(2,1)S(1)}, bf16[64,128]{1,0:T(8,128)(2,1)S(1)}, u32[]{:S(2)}, u32[]{:S(2)}) collective-permute-start(bf16[64,128]{1,0:T(8,128)(2,1)S(1)} %reduce_sum.12), channel_id=1, source_target_pairs={{0,16},{8,24},{16,0},{24,8},{32,48},{40,56},{48,32},{56,40},{64,80... | collective-permute-start | bytes 49160 | tf_op jit(solution)/shard_map/ppermute | solution.py:18
  80.7 10.3 %collective-permute-start.2 = (bf16[64,128]{1,0:T(8,128)(2,1)S(1)}, bf16[64,128]{1,0:T(8,128)(2,1)S(1)}, u32[]{:S(2)}, u32[]{:S(2)}) collective-permute-start(bf16[64,128]{1,0:T(8,128)(2,1)S(1)} %reduce_sum.12), channel_id=1, source_target_pairs={{0,32},{8,40},{16,48},{24,56},{32,0},{40,8},{48,16},{56,24},{64,96... | collective-permute-start | bytes 49160 | tf_op jit(solution)/shard_map/ppermute | solution.py:18
  85.0 6.0 %collective-permute-start.3 = (bf16[64,128]{1,0:T(8,128)(2,1)S(1)}, bf16[64,128]{1,0:T(8,128)(2,1)S(1)}, u32[]{:S(2)}, u32[]{:S(2)}) collective-permute-start(bf16[64,128]{1,0:T(8,128)(2,1)S(1)} %reduce_sum.12), channel_id=1, source_target_pairs={{0,64},{8,72},{16,80},{24,88},{32,96},{40,104},{48,112},{56,120},{... | collective-permute-start | bytes 49160 | tf_op jit(solution)/shard_map/ppermute | solution.py:18
  91.1 14.3 %copy-start.4 = (f32[64,128]{1,0:T(8,128)S(1)}, f32[64,128]{1,0:T(8,128)}, u32[]{:S(2)}) copy-start(f32[64,128]{1,0:T(8,128)} %param.17) | copy-start | bytes 98308
  231.1 18.7 %collective-permute-start.4 = (bf16[512,128]{1,0:T(8,128)(2,1)}, bf16[512,128]{1,0:T(8,128)(2,1)S(1)}, u32[]{:S(2)}, u32[]{:S(2)}) collective-permute-start(bf16[512,128]{1,0:T(8,128)(2,1)} %all-reduce.2.cloned.1.call-done), channel_id=1, source_target_pairs={{0,8},{8,0},{16,24},{24,16},{32,40},{40,32},{48,56},{56,48},{64,72... | collective-permute-start | bytes 393224 | tf_op jit(solution)/shard_map/ppermute | solution.py:18
  239.2 10.7 %collective-permute-start.5 = (bf16[512,128]{1,0:T(8,128)(2,1)}, bf16[512,128]{1,0:T(8,128)(2,1)S(1)}, u32[]{:S(2)}, u32[]{:S(2)}) collective-permute-start(bf16[512,128]{1,0:T(8,128)(2,1)} %all-reduce.2.cloned.1.call-done), channel_id=1, source_target_pairs={{0,16},{8,24},{16,0},{24,8},{32,48},{40,56},{48,32},{56,40},{64,80... | collective-permute-start | bytes 393224 | tf_op jit(solution)/shard_map/ppermute | solution.py:18
  242.3 9.1 %collective-permute-start.6 = (bf16[512,128]{1,0:T(8,128)(2,1)}, bf16[512,128]{1,0:T(8,128)(2,1)S(1)}, u32[]{:S(2)}, u32[]{:S(2)}) collective-permute-start(bf16[512,128]{1,0:T(8,128)(2,1)} %all-reduce.2.cloned.1.call-done), channel_id=1, source_target_pairs={{0,32},{8,40},{16,48},{24,56},{32,0},{40,8},{48,16},{56,24},{64,96... | collective-permute-start | bytes 393224 | tf_op jit(solution)/shard_map/ppermute | solution.py:18
  246.6 6.6 %collective-permute-start.7 = (bf16[512,128]{1,0:T(8,128)(2,1)}, bf16[512,128]{1,0:T(8,128)(2,1)S(1)}, u32[]{:S(2)}, u32[]{:S(2)}) collective-permute-start(bf16[512,128]{1,0:T(8,128)(2,1)} %all-reduce.2.cloned.1.call-done), channel_id=1, source_target_pairs={{0,64},{8,72},{16,80},{24,88},{32,96},{40,104},{48,112},{56,120},{... | collective-permute-start | bytes 393224 | tf_op jit(solution)/shard_map/ppermute | solution.py:18
  253.2 0.8 copy-start.3
  402.4 2.4 copy-start.5
Sparse Core Ops, SparseCore 0:
  87.8 143.2 all-reduce.1
